TPU v7x, 32 devices: a whole 2x2x4 slice. The times are simulated.
32 devices in a mesh: row: 8 (over z, x), col: 4 (over y, core).
Axes of the slice: x: 2, y: 2, z: 4, core: 2. Of those that a mesh axis runs over, the one named last changes fastest.
Arguments:
- pair: bfloat16 [1536, 1536, 128], P('row', 'col'), may hold values from -6 to 6
- gain_in: float32 [128], replicated, may hold values from 0.25 to 1.75
- w_a_gate: bfloat16 [128, 128], replicated, may hold values from -0.5 to 0.5
- w_a: bfloat16 [128, 128], replicated, may hold values from -0.5 to 0.5
- w_b_gate: bfloat16 [128, 128], replicated, may hold values from -0.5 to 0.5
- w_b: bfloat16 [128, 128], replicated, may hold values from -0.5 to 0.5
- w_out_gate: bfloat16 [128, 128], replicated, may hold values from -0.5 to 0.5
- w_out: bfloat16 [128, 128], replicated, may hold values from -0.5 to 0.5
- gain_out: float32 [128], replicated, may hold values from 0.25 to 1.75
Outputs:
- update: bfloat16 [1536, 1536, 128], P('row', 'col')
All inputs are finite; a program needn't handle non-finite values.
Results may differ from a plain program's by a relative error of at most 0.0083.
Values may be sent and summed in bfloat16 or wider, within the bound.
A program may use at most 256 MiB of HBM per device.

v0:
```python
import jax
import jax.numpy as jnp
from jax import lax
from jax.sharding import PartitionSpec as P


def layer_norm_last(values, gain):
    centred = values - jnp.mean(values, axis=-1, keepdims=True)
    variance = jnp.mean(centred * centred, axis=-1, keepdims=True)
    return centred * lax.rsqrt(variance + 1e-05) * gain


def project_major(normed, weight):
    return jnp.einsum("ijd,de->eij", normed, weight, preferred_element_type=jnp.float32)


def local(pair, gain_in, w_a_gate, w_a, w_b_gate, w_b, w_out_gate, w_out, gain_out):
    normed = layer_norm_last(pair.astype(jnp.float32), gain_in).astype(jnp.bfloat16)
    left = (jax.nn.sigmoid(project_major(normed, w_a_gate)) * project_major(normed, w_a)).astype(
        jnp.bfloat16
    )
    right = (jax.nn.sigmoid(project_major(normed, w_b_gate)) * project_major(normed, w_b)).astype(
        jnp.bfloat16
    )
    gating = jax.nn.sigmoid(
        jnp.einsum("ijd,de->ije", normed, w_out_gate, preferred_element_type=jnp.float32)
    )
    left_owned, right_owned = (
        lax.all_to_all(left, "row", split_axis=0, concat_axis=1, tiled=True),
        lax.all_to_all(right, "row", split_axis=0, concat_axis=1, tiled=True),
    )
    summed = jnp.einsum(
        "cki,ckj->cij",
        lax.all_gather(left_owned, "col", axis=2, tiled=True),
        right_owned,
        preferred_element_type=jnp.float32,
    ).astype(jnp.bfloat16)
    returned = lax.all_to_all(summed, "row", split_axis=1, concat_axis=0, tiled=True)
    values = returned.astype(jnp.float32)
    centred = values - jnp.mean(values, axis=0, keepdims=True)
    variance = jnp.mean(centred * centred, axis=0, keepdims=True)
    scaled = (centred * lax.rsqrt(variance + 1e-05) * gain_out[:, None, None]).astype(jnp.bfloat16)
    projected = jnp.einsum("cij,cd->ijd", scaled, w_out, preferred_element_type=jnp.float32)
    return (gating * projected).astype(jnp.bfloat16)


def solution(mesh):
    in_specs = (P("row", "col", None), P(), P(), P(), P(), P(), P(), P(), P())
    out_specs = P("row", "col", None)
    return jax.shard_map(local, mesh=mesh, in_specs=in_specs, out_specs=out_specs, check_vma=False)
```

profile of v0, /device:TPU:0, one launch (start us, length us, event | category | flops | bytes accessed | tf_op | source)
XLA Modules:
  0.0 1724.9 jit_solution(12179436073618895880)
XLA Ops:
  6.6 12.9 convert_reduce_fusion
  19.5 0.0 slice-start.3
  19.5 0.0 slice-start.4
  19.5 0.0 copy-start.11
  19.6 23.4 %fusion.2 = f32[192,384]{1,0:T(8,128)S(1)} fusion(bf16[192,384,128]{2,1,0:T(8,128)(2,1)} %param.9, f32[192,384]{1,0:T(8,128)S(1)} %broadcast_multiply_fusion.1), kind=kLoop, calls=%fused_computation.4 | loop fusion | flops 37675008 | bytes 19464192 | tf_op jit(solution)/shard_map/reduce_sum | solution.py:9
  43.1 30.1 %fusion.17 = f32[192,384,128]{2,1,0:T(8,128)} fusion(bf16[128,128]{1,0:T(8,128)(2,1)S(1)} %copy-done, bf16[192,384,128]{2,1,0:T(8,128)(2,1)S(1)} %bitcast.53, f32[128]{0:T(128)S(1)} %copy-done.6, f32[192,384]{1,0:T(8,128)S(1)} %add_rsqrt_fusion.1, f32[192,384]{1,0:T(8,128)S(1)} %broadcast_multiply_fusion.1), kind=kOutput, calls=%fused_computation.30 | convolution fusion | flops 2463105024 | bytes 57246208 | tf_op jit(solution)/shard_map/ijd,de->eij/dot_general | solution.py:14
  73.2 33.4 %fusion.11 = bf16[128,192,384]{0,2,1:T(8,128)(2,1)} fusion(f32[192,384,128]{2,1,0:T(8,128)} %fusion.17, bf16[128,128]{1,0:T(8,128)(2,1)S(1)} %copy-done.11, bf16[192,384,128]{2,1,0:T(8,128)(2,1)S(1)} %bitcast.53, f32[128]{0:T(128)S(1)} %copy-done.6, f32[192,384]{1,0:T(8,128)S(1)} %add_rsqrt_fusion.1, f32[192,384]{1,0:T(8,128)S(1)} %broadcast_multiply_fusion.1), kind=kOutput, calls=%fused_computation.19 | convolution fusion | flops 2510290944 | bytes 76120576 | tf_op jit(solution)/shard_map/ijd,de->eij/dot_general | solution.py:14
  106.6 24.4 %copy.27 = bf16[128,192,384]{2,1,0:T(8,128)(2,1)} copy(bf16[128,192,384]{0,2,1:T(8,128)(2,1)} %fusion.11) | data formatting | bytes 37748736 | tf_op jit(solution)/shard_map/convert_element_type | solution.py:19
  131.0 415.0 %all_to_all.45 = bf16[128,192,384]{2,1,0:T(8,128)(2,1)S(1)} all-to-all(bf16[128,192,384]{2,1,0:T(8,128)(2,1)} %copy.27), channel_id=1, replica_groups=mesh['row'=8,'col'=4] {'row'}, dimensions={0} | all-to-all | bytes 37748736 | tf_op jit(solution)/shard_map/all_to_all | solution.py:29
  546.0 6.9 copy.28
  552.9 24.7 %copy.29 = bf16[16,1536,384]{1,2,0:T(8,128)(2,1)} copy(bf16[16,1536,384]{2,1,0:T(8,128)(2,1)} %bitcast.58) | data formatting | bytes 37748736 | tf_op jit(solution)/shard_map/all_to_all | solution.py:29
  577.6 0.0 all-gather.2.cloned.1.call-update
  577.6 34.0 %fusion.14 = f32[192,384,128]{2,1,0:T(8,128)S(1)} fusion(bf16[128,128]{1,0:T(8,128)(2,1)S(1)} %copy-done.8, bf16[192,384,128]{2,1,0:T(8,128)(2,1)} %param.9, f32[128]{0:T(128)S(1)} %copy-done.6, f32[192,384]{1,0:T(8,128)S(1)} %add_rsqrt_fusion.1, f32[192,384]{1,0:T(8,128)S(1)} %broadcast_multiply_fusion.1), kind=kOutput, calls=%fused_computation.27 | convolution fusion | flops 2463105024 | bytes 57246208 | tf_op jit(solution)/shard_map/ijd,de->eij/dot_general | solution.py:14
  611.6 28.1 %fusion.12 = bf16[128,192,384]{0,2,1:T(8,128)(2,1)} fusion(f32[192,384,128]{2,1,0:T(8,128)S(1)} %fusion.14, bf16[128,128]{1,0:T(8,128)(2,1)S(1)} %copy-done.12, bf16[192,384,128]{2,1,0:T(8,128)(2,1)} %param.9, f32[128]{0:T(128)S(1)} %copy-done.6, f32[192,384]{1,0:T(8,128)S(1)} %add_rsqrt_fusion.1, f32[192,384]{1,0:T(8,128)S(1)} %broadcast_multiply_fusion.1), kind=kOutput, calls=%fused_computation.20 | convolution fusion | flops 2510290944 | bytes 76120576 | tf_op jit(solution)/shard_map/ijd,de->eij/dot_general | solution.py:14
  639.7 24.5 %copy.30 = bf16[128,192,384]{2,1,0:T(8,128)(2,1)} copy(bf16[128,192,384]{0,2,1:T(8,128)(2,1)} %fusion.12) | data formatting | bytes 37748736 | tf_op jit(solution)/shard_map/convert_element_type | solution.py:22
  664.2 411.5 %all_to_all.46 = bf16[128,192,384]{2,1,0:T(8,128)(2,1)S(1)} all-to-all(bf16[128,192,384]{2,1,0:T(8,128)(2,1)} %copy.30), channel_id=1, replica_groups=mesh['row'=8,'col'=4] {'row'}, dimensions={0} | all-to-all | bytes 37748736 | tf_op jit(solution)/shard_map/all_to_all | solution.py:30
  1075.7 6.9 copy.31
  1082.7 51.9 %convolution_convert_fusion = bf16[16,1536,384]{2,1,0:T(8,128)(2,1)} fusion(bf16[16,1536,1536]{1,2,0:T(8,128)(2,1)} %all-gather.2.cloned.1.call-done, bf16[16,1536,384]{2,1,0:T(8,128)(2,1)} %bitcast.60), kind=kOutput, calls=%fused_computation.21 | convolution fusion | flops 29000466432 | bytes 113246208 | tf_op jit(solution)/shard_map/cki,ckj->cij/dot_general | solution.py:32
  1134.5 16.4 copy.32
  1151.0 410.9 %all_to_all.47 = bf16[16,1536,384]{2,0,1:T(8,128)(2,1)S(1)} all-to-all(bf16[16,1536,384]{2,0,1:T(8,128)(2,1)S(1)} %copy.32), channel_id=1, replica_groups=mesh['row'=8,'col'=4] {'row'}, dimensions={1} | all-to-all | bytes 37748736 | tf_op jit(solution)/shard_map/all_to_all | solution.py:38
  1561.8 21.7 %copy.33 = bf16[16,1536,384]{2,1,0:T(8,128)(2,1)S(1)} copy(bf16[16,1536,384]{2,0,1:T(8,128)(2,1)S(1)} %all_to_all.47) | data formatting | bytes 37748736 | tf_op jit(solution)/shard_map/all_to_all | solution.py:38
  1583.6 3.4 fusion.8
  1586.9 13.2 convert_bitcast_fusion
  1600.1 5.4 multiply_reduce_fusion
  1605.6 0.0 copy-start.10
  1605.6 28.4 %copy.34 = f32[8,16,192,384]{3,2,1,0:T(8,128)} copy(f32[8,16,192,384]{3,2,0,1:T(8,128)} %convert_bitcast_fusion) | data formatting | bytes 75497472 | tf_op jit(solution)/shard_map/convert_element_type | solution.py:39
  1634.0 22.1 %fusion.7 = bf16[128,192,384]{2,1,0:T(8,128)(2,1)} fusion(f32[8,16,192,384]{3,2,1,0:T(8,128)} %copy.34, f32[128]{0:T(128)S(1)} %copy-done.10, f32[192,384]{1,0:T(8,128)S(1)} %add_rsqrt_fusion, f32[192,384]{1,0:T(8,128)S(1)} %broadcast_multiply_fusion), kind=kLoop, calls=%fused_computation.11 | loop fusion | flops 37748736 | bytes 57213440 | tf_op jit(solution)/shard_map/convert_element_type | solution.py:42
  1656.2 0.0 copy-start.7
  1656.2 0.0 copy-start.13
  1656.2 33.5 %fusion.9 = f32[192,384,128]{2,1,0:T(8,128)} fusion(bf16[128,192,384]{2,1,0:T(8,128)(2,1)} %fusion.7, bf16[128,128]{1,0:T(8,128)(2,1)S(1)} %copy-done.9), kind=kOutput, calls=%fused_computation.17 | convolution fusion | flops 2415919104 | bytes 56655872 | tf_op jit(solution)/shard_map/cij,cd->ijd/dot_general | solution.py:43
  1689.8 0.0 copy-start.1
  1689.8 28.2 %multiply_convert_fusion.2 = bf16[192,384,128]{2,1,0:T(8,128)(2,1)} fusion(f32[192,384,128]{2,1,0:T(8,128)} %fusion.9, bf16[128,128]{1,0:T(8,128)(2,1)S(1)} %copy-done.13, bf16[192,384,128]{2,1,0:T(8,128)(2,1)} %param.9, f32[128]{0:T(128)S(1)} %copy-done.7, f32[192,384]{1,0:T(8,128)S(1)} %copy-done.5, f32[192,384]{1,0:T(8,128)S(1)} %copy-done.3), kind=kOutput, calls=%fused_computation.14 | convolution fusion | flops 2510290944 | bytes 76120576 | tf_op jit(solution)/shard_map/ijd,de->ije/dot_general | solution.py:26
  (38 shorter events, 0.2 us)
Async XLA Ops:
  6.5 36.5 %copy-start = (bf16[128,128]{1,0:T(8,128)(2,1)S(1)}, bf16[128,128]{1,0:T(8,128)(2,1)}, u32[]{:S(2)}) copy-start(bf16[128,128]{1,0:T(8,128)(2,1)} %param.12) | copy-start | bytes 98308
  6.5 36.5 %copy-start.6 = (f32[128]{0:T(128)S(1)}, f32[128]{0:T(128)}, u32[]{:S(2)}) copy-start(f32[128]{0:T(128)} %param.10) | copy-start | bytes 1540
  6.5 1076.1 %all-gather.2.cloned.1.call-start = ((), (), s32[]{:S(2)}) async-start(), calls=%async_computation.3 | async-start | bytes 94371840 | tf_op jit(solution)/shard_map/all_gather | solution.py:34
  6.5 36.5 %slice-start = ((s8[18874368]{0:T(1024)(128)(4,1)}), s8[4194304]{0:T(1024)(128)(4,1)S(1)}, s32[]{:S(2)}) async-start(s8[18874368]{0:T(1024)(128)(4,1)} %bitcast.52), calls=%async_computation.4 | async-start | bytes 8388608
  6.5 36.5 %slice-start.1 = ((s8[18874368]{0:T(1024)(128)(4,1)}), s8[4194304]{0:T(1024)(128)(4,1)S(1)}, s32[]{:S(2)}) async-start(s8[18874368]{0:T(1024)(128)(4,1)} %bitcast.52), calls=%async_computation.5 | async-start | bytes 8388608
  6.6 36.5 %slice-start.2 = ((s8[18874368]{0:T(1024)(128)(4,1)}), s8[4194304]{0:T(1024)(128)(4,1)S(1)}, s32[]{:S(2)}) async-start(s8[18874368]{0:T(1024)(128)(4,1)} %bitcast.52), calls=%async_computation.6 | async-start | bytes 8388608
  19.5 592.1 %copy-start.2 = (f32[192,384]{1,0:T(8,128)}, f32[192,384]{1,0:T(8,128)S(1)}, u32[]{:S(2)}) copy-start(f32[192,384]{1,0:T(8,128)S(1)} %broadcast_multiply_fusion.1) | copy-start | bytes 884740
  19.5 23.5 %slice-start.3 = ((s8[18874368]{0:T(1024)(128)(4,1)}), s8[4194304]{0:T(1024)(128)(4,1)S(1)}, s32[]{:S(2)}) async-start(s8[18874368]{0:T(1024)(128)(4,1)} %bitcast.52), calls=%async_computation.7 | async-start | bytes 8388608
  19.5 23.5 %slice-start.4 = ((s8[18874368]{0:T(1024)(128)(4,1)}), s8[2097152]{0:T(1024)(128)(4,1)S(1)}, s32[]{:S(2)}) async-start(s8[18874368]{0:T(1024)(128)(4,1)} %bitcast.52), calls=%async_computation.8 | async-start | bytes 4194304
  19.5 53.6 %copy-start.11 = (bf16[128,128]{1,0:T(8,128)(2,1)S(1)}, bf16[128,128]{1,0:T(8,128)(2,1)}, u32[]{:S(2)}) copy-start(bf16[128,128]{1,0:T(8,128)(2,1)} %param.11) | copy-start | bytes 98308
  43.1 568.5 %copy-start.4 = (f32[192,384]{1,0:T(8,128)}, f32[192,384]{1,0:T(8,128)S(1)}, u32[]{:S(2)}) copy-start(f32[192,384]{1,0:T(8,128)S(1)} %add_rsqrt_fusion.1) | copy-start | bytes 884740
  552.9 24.7 %copy-start.8 = (bf16[128,128]{1,0:T(8,128)(2,1)S(1)}, bf16[128,128]{1,0:T(8,128)(2,1)}, u32[]{:S(2)}) copy-start(bf16[128,128]{1,0:T(8,128)(2,1)} %param.14) | copy-start | bytes 98308
  577.6 34.0 %copy-start.12 = (bf16[128,128]{1,0:T(8,128)(2,1)S(1)}, bf16[128,128]{1,0:T(8,128)(2,1)}, u32[]{:S(2)}) copy-start(bf16[128,128]{1,0:T(8,128)(2,1)} %param.13) | copy-start | bytes 98308
  1605.6 28.4 %copy-start.10 = (f32[128]{0:T(128)S(1)}, f32[128]{0:T(128)}, u32[]{:S(2)}) copy-start(f32[128]{0:T(128)} %param.17) | copy-start | bytes 1540
  1634.0 22.1 %copy-start.9 = (bf16[128,128]{1,0:T(8,128)(2,1)S(1)}, bf16[128,128]{1,0:T(8,128)(2,1)}, u32[]{:S(2)}) copy-start(bf16[128,128]{1,0:T(8,128)(2,1)} %param.16) | copy-start | bytes 98308
  1656.2 33.6 %copy-start.3 = (f32[192,384]{1,0:T(8,128)S(1)}, f32[192,384]{1,0:T(8,128)}, u32[]{:S(2)}) copy-start(f32[192,384]{1,0:T(8,128)} %copy-done.2) | copy-start | bytes 884740
  1656.2 33.6 %copy-start.5 = (f32[192,384]{1,0:T(8,128)S(1)}, f32[192,384]{1,0:T(8,128)}, u32[]{:S(2)}) copy-start(f32[192,384]{1,0:T(8,128)} %copy-done.4) | copy-start | bytes 884740
  1656.2 33.6 %copy-start.7 = (f32[128]{0:T(128)S(1)}, f32[128]{0:T(128)}, u32[]{:S(2)}) copy-start(f32[128]{0:T(128)} %param.10) | copy-start | bytes 1540
  1656.2 33.6 %copy-start.13 = (bf16[128,128]{1,0:T(8,128)(2,1)S(1)}, bf16[128,128]{1,0:T(8,128)(2,1)}, u32[]{:S(2)}) copy-start(bf16[128,128]{1,0:T(8,128)(2,1)} %param.15) | copy-start | bytes 98308
  1689.8 28.2 %copy-start.1 = (bf16[128,128]{1,0:T(8,128)(2,1)S(1)}, bf16[128,128]{1,0:T(8,128)(2,1)}, u32[]{:S(2)}) copy-start(bf16[128,128]{1,0:T(8,128)(2,1)} %param.12) | copy-start | bytes 98308
Sparse Core Ops, SparseCore 0:
  577.7 440.9 all-gather.1
where the time goes:
time: 1730 us; the launch traced here: 1720 us
  blocking collectives  1240 us (72%)
  matrix products  239 us (14%)
  local copies, waits for them, and re-layouts  154 us (9%)
  other arithmetic  80.5 us (5%)
    all_to_all x1, blocking collectives, local(): lax.all_to_all(left, 'row', split_axis=0, concat_axis=1, tiled=True)  415 us
    all_to_all x1, blocking collectives, local(): lax.all_to_all(right, 'row', split_axis=0, concat_axis=1, tiled=True)  412 us
    all_to_all x1, blocking collectives, local(): lax.all_to_all(summed, 'row', split_axis=1, concat_axis=0, tiled=True)  411 us
    dot_general x4, matrix products, project_major(): jnp.einsum('ijd,de->eij', normed, weight, preferred_element_type=jnp.floa...  126 us
    dot_general x1, matrix products, local(): jnp.einsum('cki,ckj->cij', lax.all_gather(left_owned, 'col', axis=2, tile...  51.9 us
  transfers between devices with their start and end apart: 1, of which 0 were waited for; matrix products, arithmetic and copies ran while one was open for 5% of the time, Pallas kernels for 0%

commit v1 on v0

v1 whole, which is shorter than its diff:
```python
import functools

import jax
import jax.numpy as jnp
from jax import lax
from jax.experimental import pallas as pl
from jax.experimental.pallas import tpu as pltpu
from jax.sharding import Mesh, PartitionSpec as P

BF16, F32 = jnp.bfloat16, jnp.float32
ROWS = 16
GROUP = ("rlo", "col")
VMEM_LIMIT = 56 * 1024 * 1024


def norm_last(x, gain):
    values = x.astype(F32)
    centred = values - jnp.mean(values, axis=-1, keepdims=True)
    variance = jnp.mean(centred * centred, axis=-1, keepdims=True)
    return (centred * lax.rsqrt(variance + 1e-05) * gain).astype(BF16)


def dot(a, b, da, db):
    return lax.dot_general(a, b, (((da,), (db,)), ((), ())), preferred_element_type=F32)


def gated(both):
    c = both.shape[0] // 2
    return jax.nn.sigmoid(both[:c]) * both[c:]


def front_kernel(S, M, w, x_ref, gain_ref, wl_ref, wr_ref, l0_ref, l1_ref, r0_ref, r1_ref, lscr, rscr):
    c = lscr.shape[0]
    half = c // 2

    def step(k, carry):
        xn = norm_last(x_ref[k], gain_ref[...])
        rscr[:, k, :] = gated(dot(wr_ref[...], xn, 1, 1))
        parts = [
            xn[(s * M + m) * w : (s * M + m + 1) * w] for m in range(M) for s in range(S)
        ]
        lscr[:, k, :] = gated(dot(wl_ref[...], jnp.concatenate(parts, axis=0), 1, 1))
        return carry

    lax.fori_loop(0, x_ref.shape[0], step, 0)
    width = S * w
    for q, (l_ref, r_ref) in enumerate(((l0_ref, r0_ref), (l1_ref, r1_ref))):
        r_ref[...] = rscr[q * half : (q + 1) * half].astype(BF16)
        for m in range(M):
            l_ref[m] = lscr[q * half : (q + 1) * half, :, m * width : (m + 1) * width].astype(BF16)


def front(pair, gain, wl, wr, S, M, w):
    K, J, C = pair.shape
    half, width = C // 2, S * w
    fixed = lambda i: (0, 0)
    lspec = pl.BlockSpec((M, half, ROWS, width), lambda i: (0, 0, i, 0))
    rspec = pl.BlockSpec((half, ROWS, J), lambda i: (0, i, 0))
    lshape = jax.ShapeDtypeStruct((M, half, K, width), BF16)
    rshape = jax.ShapeDtypeStruct((half, K, J), BF16)
    return pl.pallas_call(
        functools.partial(front_kernel, S, M, w),
        grid=(K // ROWS,),
        in_specs=[
            pl.BlockSpec((ROWS, J, C), lambda i: (i, 0, 0)),
            pl.BlockSpec((1, C), fixed),
            pl.BlockSpec((2 * C, C), fixed),
            pl.BlockSpec((2 * C, C), fixed),
        ],
        out_specs=[lspec, lspec, rspec, rspec],
        out_shape=[lshape, lshape, rshape, rshape],
        scratch_shapes=[pltpu.VMEM((C, ROWS, J), F32), pltpu.VMEM((C, ROWS, J), F32)],
        compiler_params=pltpu.CompilerParams(vmem_limit_bytes=VMEM_LIMIT),
        cost_estimate=pl.CostEstimate(
            flops=8 * K * J * C * C, bytes_accessed=6 * K * J * C, transcendentals=2 * K * J * C
        ),
    )(pair, gain.reshape(1, C), wl, wr)


def contract_kernel(S, w, add, which_ref, l_ref, r_ref, *rest):
    got_ref, out_ref = (rest[0], rest[-1]) if add else (None, rest[-1])
    rlo, cols, _, k, width = l_ref.shape
    ncol, J = r_ref.shape[1], r_ref.shape[4]
    lhs = jnp.concatenate(
        [l_ref[:, ci, 0].reshape(rlo * k, width) for ci in range(cols)], axis=1
    )
    lhs = lhs.T
    for cj in range(ncol):
        acc = dot(lhs, r_ref[:, cj, 0].reshape(rlo * k, J), 1, 0)
        acc = acc.reshape(cols * S, w, J)
        if add:
            acc = acc + got_ref[:, cj, 0].astype(F32)
        out_ref[:, cj, 0] = acc.astype(BF16)


def contract(which, l, r, S, w, got=None, after=None):
    rlo, ncol, g, k, width = l.shape
    J = r.shape[4]
    cols = ncol // 2
    pspec = pl.BlockSpec((cols * S, ncol, 1, w, J), lambda i, h: (0, 0, i, 0, 0))
    in_specs = [
        pl.BlockSpec((rlo, cols, 1, k, width), lambda i, h: (0, h[0], i, 0, 0)),
        pl.BlockSpec((rlo, ncol, 1, k, J), lambda i, h: (0, 0, i, 0, 0)),
    ]
    operands = [l, r]
    if got is not None:
        in_specs.append(pspec)
        operands.append(got)
    if after is not None:
        in_specs.append(pl.BlockSpec(memory_space=pl.ANY))
        operands.append(after)
    size = g * cols * width * ncol * J
    return pl.pallas_call(
        functools.partial(contract_kernel, S, w, got is not None),
        grid_spec=pltpu.PrefetchScalarGridSpec(
            num_scalar_prefetch=1, grid=(g,), in_specs=in_specs, out_specs=pspec
        ),
        out_shape=jax.ShapeDtypeStruct((cols * S, ncol, g, w, J), BF16),
        compiler_params=pltpu.CompilerParams(vmem_limit_bytes=VMEM_LIMIT),
        cost_estimate=pl.CostEstimate(
            flops=2 * size * rlo * k,
            bytes_accessed=2 * (size + r.size + l.size // 2),
            transcendentals=0,
        ),
    )(which, *operands)


def finish_kernel(v0_ref, v1_ref, x_ref, gin_ref, gout_ref, wg_ref, wo_ref, *rest):
    out_ref, scr = rest[-2], rest[-1]
    half = scr.shape[0] // 2
    scr[:half] = v0_ref[...].astype(F32)
    scr[half:] = v1_ref[...].astype(F32)

    def step(i, carry):
        values = scr[:, i, :]
        centred = values - jnp.mean(values, axis=0, keepdims=True)
        variance = jnp.mean(centred * centred, axis=0, keepdims=True)
        scaled = (centred * lax.rsqrt(variance + 1e-05) * gout_ref[...]).astype(BF16)
        projected = dot(scaled, wo_ref[...], 0, 0)
        gate = jax.nn.sigmoid(dot(norm_last(x_ref[i], gin_ref[...]), wg_ref[...], 1, 0))
        out_ref[i] = (gate * projected).astype(BF16)
        return carry

    lax.fori_loop(0, x_ref.shape[0], step, 0)


def finish(v0, v1, pair, gain_in, gain_out, wg, wo, base, before):
    K, J, C = pair.shape
    half, w, _ = v0.shape
    fixed = lambda i: (0, 0)
    vspec = pl.BlockSpec((half, ROWS, J), lambda i: (0, i, 0))
    xspec = pl.BlockSpec((ROWS, J, C), lambda i: (base // ROWS + i, 0, 0))
    in_specs = [
        vspec,
        vspec,
        xspec,
        pl.BlockSpec((1, C), fixed),
        pl.BlockSpec((C, 1), fixed),
        pl.BlockSpec((C, C), fixed),
        pl.BlockSpec((C, C), fixed),
    ]
    operands = [v0, v1, pair, gain_in.reshape(1, C), gain_out.reshape(C, 1), wg, wo]
    aliases = {}
    if before is not None:
        in_specs.append(pl.BlockSpec(memory_space=pl.ANY))
        aliases = {len(operands): 0}
        operands.append(before)
    return pl.pallas_call(
        finish_kernel,
        grid=(w // ROWS,),
        in_specs=in_specs,
        out_specs=xspec,
        out_shape=jax.ShapeDtypeStruct((K, J, C), BF16),
        scratch_shapes=[pltpu.VMEM((C, ROWS, J), F32)],
        input_output_aliases=aliases,
        compiler_params=pltpu.CompilerParams(vmem_limit_bytes=VMEM_LIMIT),
        cost_estimate=pl.CostEstimate(
            flops=4 * w * J * C * C, bytes_accessed=6 * w * J * C, transcendentals=w * J * C
        ),
    )(*operands)


def local(rlo, ncol, pair, gain_in, w_a_gate, w_a, w_b_gate, w_b, w_out_gate, w_out, gain_out):
    K, J, C = pair.shape
    D = rlo * ncol
    S = J // K
    w = 128 // S
    M = K // w
    half = C // 2
    g = half // D
    h = lax.axis_index("half").astype(jnp.int32)
    mine, other = h.reshape(1), (1 - h).reshape(1)
    swap = [(0, 1), (1, 0)]

    wl = jnp.concatenate([w_a_gate.T, w_a.T], axis=0)
    wr = jnp.concatenate([w_b_gate.T, w_b.T], axis=0)
    l0, l1, r0, r1 = front(pair, gain_in, wl, wr, S, M, w)
    lefts, rights = (l0, l1), (r0, r1)

    def spread(block):
        got = lax.all_to_all(block.reshape(D, g, K, -1), GROUP, 0, 0)
        return got.reshape(rlo, ncol, g, K, -1)

    def tie(value, after):
        return value if after is None else lax.optimization_barrier((value, after))[0]

    items = [(q, m) for q in range(2) for m in range(M)]
    held_r, held_l, came, back = {}, {}, {}, {}
    out = None

    def prepare(t, after):
        q, m = items[t]
        if q not in held_r:
            held_r[q] = spread(tie(rights[q], after))
        held_l[t] = spread(tie(lefts[q][m], after))
        sent = contract(other, held_l[t], held_r[q], S, w)
        came[t] = lax.ppermute(sent, "half", swap)
        return sent

    def consume(t, after):
        nonlocal out
        q, m = items[t]
        total = contract(mine, held_l.pop(t), held_r[q], S, w, came.pop(t), after)
        ret = lax.all_to_all(total.reshape(D, g, w, J), GROUP, 0, 0)
        back[t] = ret.reshape(half, w, J)
        if q == 1:
            out = finish(
                back.pop(m), back.pop(t), pair, gain_in, gain_out, w_out_gate, w_out, m * w, out
            )
        return total

    last = prepare(0, None)
    last = prepare(1, last)
    held_r[1] = spread(tie(rights[1], last))
    for t in range(len(items)):
        done = consume(t, last)
        if t + 2 < len(items):
            last = prepare(t + 2, done)
        else:
            last = None
    return out


def solution(mesh):
    rows, ncol = mesh.shape["row"], mesh.shape["col"]
    split = Mesh(mesh.devices.reshape(2, rows // 2, ncol), ("half", "rlo", "col"))
    spec = P(("half", "rlo"), "col", None)
    in_specs = (spec, P(), P(), P(), P(), P(), P(), P(), P())
    return jax.shard_map(
        functools.partial(local, rows // 2, ncol),
        mesh=split,
        in_specs=in_specs,
        out_specs=spec,
        check_vma=False,
    )
```

time: 1730 us -> 1640 us (0.948)
  blocking collectives: 1240 us -> 286 us
  waiting for transfers between devices: 0.02 us -> 950 us
  Pallas kernels: 0 us -> 317 us
  matrix products: 239 us -> 0 us
  local copies, waits for them, and re-layouts: 154 us -> 31.8 us
  other arithmetic: 80.5 us -> 0.67 us
  starting transfers between devices: 0.01 us -> 57.8 us
    all_to_all x3 -> x5, blocking collectives: 1240 us -> 286 us  [spread(): got = lax.all_to_all(block.reshape(D, g, K, -1), GROUP, 0, 0)]
    ppermute x0 -> x6, waiting for transfers between devices: none -> 693 us  [prepare(): came[t] = lax.ppermute(sent, 'half', swap)]
    pallas_call x0 -> x16, Pallas kernels: none -> 317 us  [the longest x1 115 us: front(): pl.pallas_call(functools.partial(front_kernel, S, M, w), grid=(K // ROWS,...]
    all_to_all x0 -> x9, waiting for transfers between devices: none -> 257 us  [the longest x3 257 us: spread(): got = lax.all_to_all(block.reshape(D, g, K, -1), GROUP, 0, 0)]
    dot_general x7 -> x0, matrix products: 239 us -> none  [the longest x4 126 us: project_major(): jnp.einsum('ijd,de->eij', normed, weight, preferred_element_type=jnp.floa...]
    convert_element_type x4 -> x0, local copies, waits for them, and re-layouts: 93.7 us -> none  [the longest x1 28.4 us: local(): values = returned.astype(jnp.float32)]
    all_to_all x4 -> x0, local copies, waits for them, and re-layouts: 60.3 us -> none  [the longest x2 31.6 us: local(): lax.all_to_all(left, 'row', split_axis=0, concat_axis=1, tiled=True)]
    reduce_sum x4 -> x0, other arithmetic: 45.1 us -> none  [the longest x1 23.4 us: layer_norm_last(): variance = jnp.mean(centred * centred, axis=-1, keepdims=True)]
  transfers between devices with their start and end apart: 1 -> 15, of which waited for: 0 -> 9; matrix products, arithmetic and copies ran while one was open for 5% -> 0% of each run, Pallas kernels for 0% -> 9%
where the time goes in v1:
time: 1640 us
  waiting for transfers between devices  950 us (58%)
  Pallas kernels  317 us (19%)
  blocking collectives  286 us (17%)
  starting transfers between devices  57.8 us (4%)
  local copies, waits for them, and re-layouts  31.8 us (2%)
    ppermute x6, waiting for transfers between devices, prepare(): came[t] = lax.ppermute(sent, 'half', swap)  693 us
    all_to_all x5, blocking collectives, spread(): got = lax.all_to_all(block.reshape(D, g, K, -1), GROUP, 0, 0)  286 us
    all_to_all x3, waiting for transfers between devices, spread(): got = lax.all_to_all(block.reshape(D, g, K, -1), GROUP, 0, 0)  257 us
    pallas_call x1, Pallas kernels, front(): pl.pallas_call(functools.partial(front_kernel, S, M, w), grid=(K // ROWS,...  115 us
    pallas_call x3, Pallas kernels, finish(): pl.pallas_call(finish_kernel, grid=(w // ROWS,), in_specs=in_specs, out_s...  101 us
    pallas_call x12, Pallas kernels, contract(): pl.pallas_call(functools.partial(contract_kernel, S, w, got is not None),...  101 us
  transfers between devices with their start and end apart: 15, of which 9 were waited for; matrix products, arithmetic and copies ran while one was open for 0% of the time, Pallas kernels for 9%

profile of v1, /device:TPU:0, one launch (start us, length us, event | category | flops | bytes accessed | tf_op | source)
XLA Modules:
  0.0 1643.4 jit_solution(10349461304542786813)
XLA Ops:
  4.2 114.6 %shard_map.91 = (bf16[3,64,192,128]{3,2,1,0:T(8,128)(2,1)}, bf16[3,64,192,128]{3,2,1,0:T(8,128)(2,1)}, bf16[64,192,384]{2,1,0:T(8,128)(2,1)}, bf16[64,192,384]{2,1,0:T(8,128)(2,1)}) custom-call(bf16[192,384,128]{2,1,0:T(8,128)(2,1)} %x_ref.7, f32[1,128]{1,0:T(1,128)} %bitcast.87, bf16[256,128]{1,0:T(8,128)(2,1)} %get-tuple-element.31.wl_ref, ...), custom_call_target="tpu_custom_call" | custom-call | flops 9663676416 | bytes 56623104 | tf_op jit(solution)/shard_map/pallas_call | solution.py:61
  118.7 5.8 slice_bitcast_fusion.3
  124.5 44.8 %all_to_all.70 = bf16[16,4,192,128]{3,2,1,0:T(8,128)(2,1)} all-to-all(bf16[16,4,192,128]{3,2,1,0:T(8,128)(2,1)S(1)} %bitcast.79), channel_id=1, replica_groups=mesh['half'=2,'rlo'=4,'col'=4] {'rlo','col'}, dimensions={0} | all-to-all | bytes 6291456 | tf_op jit(solution)/shard_map/all_to_all | solution.py:201
  174.2 138.0 %all-to-all-done.1 = bf16[16,4,192,384]{3,2,1,0:T(8,128)(2,1)} async-done(((bf16[16,4,192,384]{3,2,1,0:T(8,128)(2,1)}), bf16[16,4,192,384]{3,2,1,0:T(8,128)(2,1)}, u32[]{:S(2)}, u32[]{:S(2)}) %all-to-all-start.1) | async-done | bytes 9437216 | tf_op jit(solution)/shard_map/all_to_all | solution.py:201
  312.2 8.1 shard_map.92
  328.4 75.5 %all-to-all-done.2 = bf16[16,4,192,128]{3,2,1,0:T(8,128)(2,1)S(1)} async-done(((bf16[16,4,192,128]{3,2,1,0:T(8,128)(2,1)}), bf16[16,4,192,128]{3,2,1,0:T(8,128)(2,1)S(1)}, u32[]{:S(2)}, u32[]{:S(2)}) %all-to-all-start.2) | async-done | bytes 3145760 | tf_op jit(solution)/shard_map/all_to_all | solution.py:201
  405.6 8.1 shard_map.93.rest_1_
  413.7 51.1 %collective-permute-done.rest_0_ = bf16[4,4,4,64,384]{4,3,2,1,0:T(8,128)(2,1)} collective-permute-done((bf16[4,4,4,64,384]{4,3,2,1,0:T(8,128)(2,1)}, bf16[4,4,4,64,384]{4,3,2,1,0:T(8,128)(2,1)}, u32[]{:S(2)}, u32[]{:S(2)}) %collective-permute-start) | collective-permute-done | bytes 3145760 | tf_op jit(solution)/shard_map/ppermute | solution.py:217
  464.8 8.8 shard_map.94
  473.7 42.6 %all_to_all.71 = bf16[16,4,192,128]{3,2,1,0:T(8,128)(2,1)} all-to-all(bf16[16,4,192,128]{3,2,1,0:T(8,128)(2,1)S(1)} %bitcast.71), channel_id=1, replica_groups=mesh['half'=2,'rlo'=4,'col'=4] {'rlo','col'}, dimensions={0} | all-to-all | bytes 6291456 | tf_op jit(solution)/shard_map/all_to_all | solution.py:201
  523.5 6.7 slice_bitcast_fusion
  530.2 8.1 shard_map.95.rest_1_
  538.3 121.3 %collective-permute-done.2.rest_0_ = bf16[4,4,4,64,384]{4,3,2,1,0:T(8,128)(2,1)S(1)} collective-permute-done((bf16[4,4,4,64,384]{4,3,2,1,0:T(8,128)(2,1)}, bf16[4,4,4,64,384]{4,3,2,1,0:T(8,128)(2,1)S(1)}, u32[]{:S(2)}, u32[]{:S(2)}) %collective-permute-start.2) | collective-permute-done | bytes 3145760 | tf_op jit(solution)/shard_map/ppermute | solution.py:217
  661.3 8.6 shard_map.96
  675.9 43.5 %all-to-all-done.4 = bf16[16,4,192,128]{3,2,1,0:T(8,128)(2,1)S(1)} async-done(((bf16[16,4,192,128]{3,2,1,0:T(8,128)(2,1)}), bf16[16,4,192,128]{3,2,1,0:T(8,128)(2,1)S(1)}, u32[]{:S(2)}, u32[]{:S(2)}) %all-to-all-start.4) | async-done | bytes 3145760 | tf_op jit(solution)/shard_map/all_to_all | solution.py:201
  719.5 112.8 %all_to_all.72 = bf16[16,4,192,384]{3,2,1,0:T(8,128)(2,1)} all-to-all(bf16[16,4,192,384]{3,2,1,0:T(8,128)(2,1)} %bitcast.81), channel_id=1, replica_groups=mesh['half'=2,'rlo'=4,'col'=4] {'rlo','col'}, dimensions={0} | all-to-all | bytes 18874368 | tf_op jit(solution)/shard_map/all_to_all | solution.py:201
  839.3 8.1 shard_map.97.rest_1_
  847.5 128.0 %collective-permute-done.1.rest_0_ = bf16[4,4,4,64,384]{4,3,2,1,0:T(8,128)(2,1)S(1)} collective-permute-done((bf16[4,4,4,64,384]{4,3,2,1,0:T(8,128)(2,1)}, bf16[4,4,4,64,384]{4,3,2,1,0:T(8,128)(2,1)S(1)}, u32[]{:S(2)}, u32[]{:S(2)}) %collective-permute-start.1) | collective-permute-done | bytes 3145760 | tf_op jit(solution)/shard_map/ppermute | solution.py:217
  977.2 8.7 shard_map.98
  985.8 43.1 %all_to_all.73 = bf16[16,4,192,128]{3,2,1,0:T(8,128)(2,1)} all-to-all(bf16[16,4,192,128]{3,2,1,0:T(8,128)(2,1)} %bitcast.69), channel_id=1, replica_groups=mesh['half'=2,'rlo'=4,'col'=4] {'rlo','col'}, dimensions={0} | all-to-all | bytes 6291456 | tf_op jit(solution)/shard_map/all_to_all | solution.py:201
  1036.2 8.1 shard_map.99.rest_1_
  1044.3 127.9 %collective-permute-done.3.rest_0_ = bf16[4,4,4,64,384]{4,3,2,1,0:T(8,128)(2,1)S(1)} collective-permute-done((bf16[4,4,4,64,384]{4,3,2,1,0:T(8,128)(2,1)}, bf16[4,4,4,64,384]{4,3,2,1,0:T(8,128)(2,1)S(1)}, u32[]{:S(2)}, u32[]{:S(2)}) %collective-permute-start.3) | collective-permute-done | bytes 3145760 | tf_op jit(solution)/shard_map/ppermute | solution.py:217
  1173.9 8.7 shard_map.100
  1182.5 43.1 %all_to_all.74 = bf16[16,4,192,128]{3,2,1,0:T(8,128)(2,1)} all-to-all(bf16[16,4,192,128]{3,2,1,0:T(8,128)(2,1)} %bitcast.68), channel_id=1, replica_groups=mesh['half'=2,'rlo'=4,'col'=4] {'rlo','col'}, dimensions={0} | all-to-all | bytes 6291456 | tf_op jit(solution)/shard_map/all_to_all | solution.py:201
  1232.7 8.1 shard_map.101.rest_1_
  1240.8 128.1 %collective-permute-done.5.rest_0_ = bf16[4,4,4,64,384]{4,3,2,1,0:T(8,128)(2,1)S(1)} collective-permute-done((bf16[4,4,4,64,384]{4,3,2,1,0:T(8,128)(2,1)}, bf16[4,4,4,64,384]{4,3,2,1,0:T(8,128)(2,1)S(1)}, u32[]{:S(2)}, u32[]{:S(2)}) %collective-permute-start.5) | collective-permute-done | bytes 3145760 | tf_op jit(solution)/shard_map/ppermute | solution.py:217
  1370.5 8.7 shard_map.103
  1388.5 136.3 %collective-permute-done.4.rest_0_ = bf16[4,4,4,64,384]{4,3,2,1,0:T(8,128)(2,1)S(1)} collective-permute-done((bf16[4,4,4,64,384]{4,3,2,1,0:T(8,128)(2,1)}, bf16[4,4,4,64,384]{4,3,2,1,0:T(8,128)(2,1)S(1)}, u32[]{:S(2)}, u32[]{:S(2)}) %collective-permute-start.4) | collective-permute-done | bytes 3145760 | tf_op jit(solution)/shard_map/ppermute | solution.py:217
  1526.5 8.6 shard_map.102
  1542.0 33.8 %shard_map.104.rest_0_ = bf16[192,384,128]{2,1,0:T(8,128)(2,1)} custom-call(bf16[64,64,384]{2,1,0:T(8,128)(2,1)} %bitcast.67, bf16[64,64,384]{2,1,0:T(8,128)(2,1)} %bitcast.70, bf16[192,384,128]{2,1,0:T(8,128)(2,1)} %x_ref.7, f32[1,128]{1,0:T(1,128)} %bitcast.88, f32[128,1]{1,0:T(8,128)} %copy.18.gout_ref, bf16[128,128]{1,0:T(8,128)(2,1)} %wg_ref.5, ...), custom_call_target="tpu_custom_call" | custom-call | flops 1610612736 | bytes 18874368 | tf_op jit(solution)/shard_map/pallas_call | solution.py:168
  1575.7 33.8 %shard_map.105.rest_0_ = bf16[192,384,128]{2,1,0:T(8,128)(2,1)} custom-call(bf16[64,64,384]{2,1,0:T(8,128)(2,1)} %bitcast.64, bf16[64,64,384]{2,1,0:T(8,128)(2,1)} %bitcast.66, bf16[192,384,128]{2,1,0:T(8,128)(2,1)} %x_ref.7, f32[1,128]{1,0:T(1,128)} %bitcast.89, f32[128,1]{1,0:T(8,128)} %copy.18.gout_ref, ...), custom_call_target="tpu_custom_call", output_to_operand_aliasing={{}: (7, {})} | custom-call | flops 1610612736 | bytes 18874368 | tf_op jit(solution)/shard_map/pallas_call | solution.py:168
  1609.6 33.8 %shard_map.106 = bf16[192,384,128]{2,1,0:T(8,128)(2,1)} custom-call(bf16[64,64,384]{2,1,0:T(8,128)(2,1)} %bitcast.65, bf16[64,64,384]{2,1,0:T(8,128)(2,1)} %bitcast.31.v1_ref, bf16[192,384,128]{2,1,0:T(8,128)(2,1)} %x_ref.7, f32[1,128]{1,0:T(1,128)} %bitcast.90, f32[128,1]{1,0:T(8,128)} %copy.18.gout_ref, ...), custom_call_target="tpu_custom_call", output_to_operand_aliasing={{}: (7, {})} | custom-call | flops 1610612736 | bytes 18874368 | tf_op jit(solution)/shard_map/pallas_call | solution.py:168
  (55 shorter events, 77.7 us)
Async XLA Ops:
  169.3 142.8 %all-to-all-start.1 = ((bf16[16,4,192,384]{3,2,1,0:T(8,128)(2,1)}), bf16[16,4,192,384]{3,2,1,0:T(8,128)(2,1)}, u32[]{:S(2)}, u32[]{:S(2)}) async-start(bf16[16,4,192,384]{3,2,1,0:T(8,128)(2,1)} %bitcast.82), calls=%async_computation.1 | async-start | bytes 18874368 | tf_op jit(solution)/shard_map/all_to_all | solution.py:201
  320.3 83.7 %all-to-all-start.2 = ((bf16[16,4,192,128]{3,2,1,0:T(8,128)(2,1)}), bf16[16,4,192,128]{3,2,1,0:T(8,128)(2,1)S(1)}, u32[]{:S(2)}, u32[]{:S(2)}) async-start(bf16[16,4,192,128]{3,2,1,0:T(8,128)(2,1)} %bitcast.73), calls=%async_computation.2 | async-start | bytes 6291456 | tf_op jit(solution)/shard_map/all_to_all | solution.py:201
  325.7 139.1 %collective-permute-start = (bf16[4,4,4,64,384]{4,3,2,1,0:T(8,128)(2,1)}, bf16[4,4,4,64,384]{4,3,2,1,0:T(8,128)(2,1)}, u32[]{:S(2)}, u32[]{:S(2)}) collective-permute-start(bf16[4,4,4,64,384]{4,3,2,1,0:T(8,128)(2,1)} %shard_map.92), channel_id=1, source_target_pairs={{0,16},{16,0},{1,17},{17,1},{2,18},{18,2},{3,19},{19,3},{4,20},{20... | collective-permute-start | bytes 9437192 | tf_op jit(solution)/shard_map/ppermute | solution.py:217
  403.9 1.7 copy-start.1
  464.8 8.8 copy-start.7
  516.3 153.7 %all-to-all-start.12 = ((bf16[16,4,64,384]{3,2,1,0:T(8,128)(2,1)}), bf16[16,4,64,384]{3,2,1,0:T(8,128)(2,1)S(1)}, u32[]{:S(2)}, u32[]{:S(2)}) async-start(bf16[16,4,64,384]{3,2,1,0:T(8,128)(2,1)} %bitcast.76), calls=%async_computation.12 | async-start | bytes 6291456 | tf_op jit(solution)/shard_map/all_to_all | solution.py:224
  520.0 139.6 %collective-permute-start.2 = (bf16[4,4,4,64,384]{4,3,2,1,0:T(8,128)(2,1)}, bf16[4,4,4,64,384]{4,3,2,1,0:T(8,128)(2,1)S(1)}, u32[]{:S(2)}, u32[]{:S(2)}) collective-permute-start(bf16[4,4,4,64,384]{4,3,2,1,0:T(8,128)(2,1)} %shard_map.93.rest_1_), channel_id=1, source_target_pairs={{0,16},{16,0},{1,17},{17,1},{2,18},{18,2},{3,19},{19,3},{4,20},{20... | collective-permute-start | bytes 9437192 | tf_op jit(solution)/shard_map/ppermute | solution.py:217
  659.6 1.7 copy-start.8
  669.9 1.7 copy-start.5
  671.6 47.9 %all-to-all-start.4 = ((bf16[16,4,192,128]{3,2,1,0:T(8,128)(2,1)}), bf16[16,4,192,128]{3,2,1,0:T(8,128)(2,1)S(1)}, u32[]{:S(2)}, u32[]{:S(2)}) async-start(bf16[16,4,192,128]{3,2,1,0:T(8,128)(2,1)} %bitcast.78), calls=%async_computation.4 | async-start | bytes 6291456 | tf_op jit(solution)/shard_map/all_to_all | solution.py:201
  719.5 112.8 %copy-start = (bf16[16,4,192,128]{3,2,1,0:T(8,128)(2,1)}, bf16[16,4,192,128]{3,2,1,0:T(8,128)(2,1)S(1)}, u32[]{:S(2)}) copy-start(bf16[16,4,192,128]{3,2,1,0:T(8,128)(2,1)S(1)} %all-to-all-done.4) | copy-start | bytes 9437188
  832.3 153.6 %all-to-all-start.10 = ((bf16[16,4,64,384]{3,2,1,0:T(8,128)(2,1)}), bf16[16,4,64,384]{3,2,1,0:T(8,128)(2,1)S(1)}, u32[]{:S(2)}, u32[]{:S(2)}) async-start(bf16[16,4,64,384]{3,2,1,0:T(8,128)(2,1)} %bitcast.72), calls=%async_computation.10 | async-start | bytes 6291456 | tf_op jit(solution)/shard_map/all_to_all | solution.py:224
  836.0 139.5 %collective-permute-start.1 = (bf16[4,4,4,64,384]{4,3,2,1,0:T(8,128)(2,1)}, bf16[4,4,4,64,384]{4,3,2,1,0:T(8,128)(2,1)S(1)}, u32[]{:S(2)}, u32[]{:S(2)}) collective-permute-start(bf16[4,4,4,64,384]{4,3,2,1,0:T(8,128)(2,1)} %shard_map.95.rest_1_), channel_id=1, source_target_pairs={{0,16},{16,0},{1,17},{17,1},{2,18},{18,2},{3,19},{19,3},{4,20},{20... | collective-permute-start | bytes 9437192 | tf_op jit(solution)/shard_map/ppermute | solution.py:217
  975.5 1.7 copy-start.9
  985.8 43.1 %copy-start.2 = (bf16[16,4,64,384]{3,2,1,0:T(8,128)(2,1)}, bf16[16,4,64,384]{3,2,1,0:T(8,128)(2,1)S(1)}, u32[]{:S(2)}) copy-start(bf16[16,4,64,384]{3,2,1,0:T(8,128)(2,1)S(1)} %all-to-all-done.10) | copy-start | bytes 9437188
  1029.0 153.6 %all-to-all-start.6 = ((bf16[16,4,64,384]{3,2,1,0:T(8,128)(2,1)}), bf16[16,4,64,384]{3,2,1,0:T(8,128)(2,1)S(1)}, u32[]{:S(2)}, u32[]{:S(2)}) async-start(bf16[16,4,64,384]{3,2,1,0:T(8,128)(2,1)} %bitcast.74), calls=%async_computation.6 | async-start | bytes 6291456 | tf_op jit(solution)/shard_map/all_to_all | solution.py:224
  1032.9 139.3 %collective-permute-start.3 = (bf16[4,4,4,64,384]{4,3,2,1,0:T(8,128)(2,1)}, bf16[4,4,4,64,384]{4,3,2,1,0:T(8,128)(2,1)S(1)}, u32[]{:S(2)}, u32[]{:S(2)}) collective-permute-start(bf16[4,4,4,64,384]{4,3,2,1,0:T(8,128)(2,1)} %shard_map.97.rest_1_), channel_id=1, source_target_pairs={{0,16},{16,0},{1,17},{17,1},{2,18},{18,2},{3,19},{19,3},{4,20},{20... | collective-permute-start | bytes 9437192 | tf_op jit(solution)/shard_map/ppermute | solution.py:217
  1172.2 1.7 copy-start.11
  1182.5 43.1 %copy-start.3 = (bf16[16,4,64,384]{3,2,1,0:T(8,128)(2,1)}, bf16[16,4,64,384]{3,2,1,0:T(8,128)(2,1)S(1)}, u32[]{:S(2)}) copy-start(bf16[16,4,64,384]{3,2,1,0:T(8,128)(2,1)S(1)} %all-to-all-done.6) | copy-start | bytes 9437188
  1225.7 153.5 %all-to-all-start.13 = ((bf16[16,4,64,384]{3,2,1,0:T(8,128)(2,1)}), bf16[16,4,64,384]{3,2,1,0:T(8,128)(2,1)S(1)}, u32[]{:S(2)}, u32[]{:S(2)}) async-start(bf16[16,4,64,384]{3,2,1,0:T(8,128)(2,1)} %bitcast.75), calls=%async_computation.13 | async-start | bytes 6291456 | tf_op jit(solution)/shard_map/all_to_all | solution.py:224
  1229.4 139.4 %collective-permute-start.5 = (bf16[4,4,4,64,384]{4,3,2,1,0:T(8,128)(2,1)}, bf16[4,4,4,64,384]{4,3,2,1,0:T(8,128)(2,1)S(1)}, u32[]{:S(2)}, u32[]{:S(2)}) collective-permute-start(bf16[4,4,4,64,384]{4,3,2,1,0:T(8,128)(2,1)} %shard_map.99.rest_1_), channel_id=1, source_target_pairs={{0,16},{16,0},{1,17},{17,1},{2,18},{18,2},{3,19},{19,3},{4,20},{20... | collective-permute-start | bytes 9437192 | tf_op jit(solution)/shard_map/ppermute | solution.py:217
  1368.8 1.6 copy-start.10
  1379.2 1.7 copy-start.6
  1380.9 154.2 %all-to-all-start.11 = ((bf16[16,4,64,384]{3,2,1,0:T(8,128)(2,1)}), bf16[16,4,64,384]{3,2,1,0:T(8,128)(2,1)S(1)}, u32[]{:S(2)}, u32[]{:S(2)}) async-start(bf16[16,4,64,384]{3,2,1,0:T(8,128)(2,1)} %bitcast.77), calls=%async_computation.11 | async-start | bytes 6291456 | tf_op jit(solution)/shard_map/all_to_all | solution.py:224
  1385.2 139.6 %collective-permute-start.4 = (bf16[4,4,4,64,384]{4,3,2,1,0:T(8,128)(2,1)}, bf16[4,4,4,64,384]{4,3,2,1,0:T(8,128)(2,1)S(1)}, u32[]{:S(2)}, u32[]{:S(2)}) collective-permute-start(bf16[4,4,4,64,384]{4,3,2,1,0:T(8,128)(2,1)} %shard_map.101.rest_1_), channel_id=1, source_target_pairs={{0,16},{16,0},{1,17},{17,1},{2,18},{18,2},{3,19},{19,3},{4,20},{20... | collective-permute-start | bytes 9437192 | tf_op jit(solution)/shard_map/ppermute | solution.py:217
  1524.8 1.7 copy-start.12
  1535.1 1.6 copy-start.4
  1535.1 6.1 copy-start.13
  1536.7 72.8 %all-to-all-start.9 = ((bf16[16,4,64,384]{3,2,1,0:T(8,128)(2,1)}), bf16[16,4,64,384]{3,2,1,0:T(8,128)(2,1)}, u32[]{:S(2)}, u32[]{:S(2)}) async-start(bf16[16,4,64,384]{3,2,1,0:T(8,128)(2,1)} %bitcast.80), calls=%async_computation.9 | async-start | bytes 6291456 | tf_op jit(solution)/shard_map/all_to_all | solution.py:224

commit v2 on v1

--- a/solution.py
+++ b/solution.py
@@ -29,10 +29,136 @@
     return jax.nn.sigmoid(both[:c]) * both[c:]
 
 
-def front_kernel(S, M, w, x_ref, gain_ref, wl_ref, wr_ref, l0_ref, l1_ref, r0_ref, r1_ref, lscr, rscr):
-    c = lscr.shape[0]
-    half = c // 2
-
+def transfers(kinds, srcs, dsts, send, recv, own):
+    h, rlo, col = (lax.axis_index(name) for name in ("half", "rlo", "col"))
+    nlo, ncol = lax.axis_size("rlo"), lax.axis_size("col")
+    D = nlo * ncol
+    me = rlo * ncol + col
+    mesh_id = pl.DeviceIdType.MESH
+    across = (1 - h, rlo, col)
+    has_swap = "swap" in kinds
+    has_spread = "spread" in kinds
+
+    def peer(step):
+        return lax.rem(me + step, D)
+
+    def place(p):
+        return (h, p // ncol, lax.rem(p, ncol))
+
+    def spread(n, step):
+        return pltpu.make_async_remote_copy(
+            src_ref=srcs[n].at[peer(step)],
+            dst_ref=dsts[n].at[me],
+            send_sem=send.at[n, step],
+            recv_sem=recv.at[n, step],
+            device_id=place(peer(step)),
+            device_id_type=mesh_id,
+        )
+
+    def swap(n):
+        return pltpu.make_async_remote_copy(
+            src_ref=srcs[n],
+            dst_ref=dsts[n],
+            send_sem=send.at[n, 0],
+            recv_sem=recv.at[n, 0],
+            device_id=across,
+            device_id_type=mesh_id,
+        )
+
+    def keep(n):
+        return pltpu.make_async_copy(srcs[n].at[me], dsts[n].at[me], own.at[n])
+
+    def begin():
+        barrier = pltpu.get_barrier_semaphore()
+        count = 0
+        if has_swap:
+            pl.semaphore_signal(barrier, inc=1, device_id=across, device_id_type=mesh_id)
+            count += 1
+        if has_spread:
+            def greet(step, carry):
+                pl.semaphore_signal(
+                    barrier, inc=1, device_id=place(peer(step)), device_id_type=mesh_id
+                )
+                return carry
+
+            lax.fori_loop(1, D, greet, 0)
+            count += D - 1
+        pl.semaphore_wait(barrier, count)
+        for n, kind in enumerate(kinds):
+            if kind == "swap":
+                swap(n).start()
+        for n, kind in enumerate(kinds):
+            if kind == "spread":
+                keep(n).start()
+
+                def go(step, carry):
+                    spread(n, step).start()
+                    return carry
+
+                lax.fori_loop(1, D, go, 0)
+
+    def end():
+        for n, kind in enumerate(kinds):
+            if kind == "spread":
+                keep(n).wait()
+
+                def settle(step, carry):
+                    spread(n, step).wait()
+                    return carry
+
+                lax.fori_loop(1, D, settle, 0)
+        for n, kind in enumerate(kinds):
+            if kind == "swap":
+                swap(n).wait()
+
+    return begin, end
+
+
+def call(kernel, grid, in_specs, out_specs, out_shapes, scratch, operands, comm, cid, aliases=None):
+    kinds = [kind for kind, _ in comm]
+    srcs = [src for _, src in comm]
+    n, n_in, n_out, n_scr = len(comm), len(operands), len(out_shapes), len(scratch)
+    anywhere = pl.BlockSpec(memory_space=pl.ANY)
+    aliases = aliases or {}
+    D = lax.axis_size("rlo") * lax.axis_size("col")
+    sems = []
+    if n:
+        sems = [
+            pltpu.SemaphoreType.DMA((n, D)),
+            pltpu.SemaphoreType.DMA((n, D)),
+            pltpu.SemaphoreType.DMA((n,)),
+        ]
+
+    def body(*refs):
+        ins, rest = refs[:n_in], refs[n_in:]
+        src_refs, rest = rest[:n], rest[n:]
+        outs, rest = rest[:n_out], rest[n_out:]
+        dst_refs, rest = rest[:n], rest[n:]
+        scr, sem = rest[:n_scr], rest[n_scr:]
+        if n:
+            begin, end = transfers(kinds, src_refs, dst_refs, *sem)
+            pl.when(pl.program_id(0) == 0)(begin)
+        if kernel is not None:
+            kernel(*ins, *outs, *scr)
+        if n:
+            pl.when(pl.program_id(0) == grid[0] - 1)(end)
+
+    params = dict(vmem_limit_bytes=VMEM_LIMIT)
+    if n:
+        params.update(collective_id=cid, has_side_effects=True)
+    return pl.pallas_call(
+        body,
+        grid=grid,
+        in_specs=[*in_specs, *[anywhere] * n],
+        out_specs=[*out_specs, *[anywhere] * n],
+        out_shape=[*out_shapes, *[jax.ShapeDtypeStruct(x.shape, x.dtype) for x in srcs]],
+        scratch_shapes=[*scratch, *sems],
+        input_output_aliases=aliases,
+        compiler_params=pltpu.CompilerParams(**params),
+    )(*operands, *srcs)
+
+
+def front_kernel(S, M, w, x_ref, gain_ref, wl_ref, wr_ref, l_ref, r_ref, lscr, rscr):
     def step(k, carry):
         xn = norm_last(x_ref[k], gain_ref[...])
         rscr[:, k, :] = gated(dot(wr_ref[...], xn, 1, 1))
@@ -44,37 +170,37 @@
 
     lax.fori_loop(0, x_ref.shape[0], step, 0)
     width = S * w
-    for q, (l_ref, r_ref) in enumerate(((l0_ref, r0_ref), (l1_ref, r1_ref))):
-        r_ref[...] = rscr[q * half : (q + 1) * half].astype(BF16)
-        for m in range(M):
-            l_ref[m] = lscr[q * half : (q + 1) * half, :, m * width : (m + 1) * width].astype(BF16)
-
-
-def front(pair, gain, wl, wr, S, M, w):
+    r_ref[...] = rscr[...].astype(BF16)
+    for m in range(M):
+        l_ref[m] = lscr[:, :, m * width : (m + 1) * width].astype(BF16)
+
+
+def front(pair, gain, wl, wr, S, M, w, comm=(), cid=None):
     K, J, C = pair.shape
     half, width = C // 2, S * w
     fixed = lambda i: (0, 0)
-    lspec = pl.BlockSpec((M, half, ROWS, width), lambda i: (0, 0, i, 0))
-    rspec = pl.BlockSpec((half, ROWS, J), lambda i: (0, i, 0))
-    lshape = jax.ShapeDtypeStruct((M, half, K, width), BF16)
-    rshape = jax.ShapeDtypeStruct((half, K, J), BF16)
-    return pl.pallas_call(
+    return call(
         functools.partial(front_kernel, S, M, w),
-        grid=(K // ROWS,),
-        in_specs=[
+        (K // ROWS,),
+        [
             pl.BlockSpec((ROWS, J, C), lambda i: (i, 0, 0)),
             pl.BlockSpec((1, C), fixed),
-            pl.BlockSpec((2 * C, C), fixed),
-            pl.BlockSpec((2 * C, C), fixed),
+            pl.BlockSpec((C, C), fixed),
+            pl.BlockSpec((C, C), fixed),
         ],
-        out_specs=[lspec, lspec, rspec, rspec],
-        out_shape=[lshape, lshape, rshape, rshape],
-        scratch_shapes=[pltpu.VMEM((C, ROWS, J), F32), pltpu.VMEM((C, ROWS, J), F32)],
-        compiler_params=pltpu.CompilerParams(vmem_limit_bytes=VMEM_LIMIT),
-        cost_estimate=pl.CostEstimate(
-            flops=8 * K * J * C * C, bytes_accessed=6 * K * J * C, transcendentals=2 * K * J * C
-        ),
-    )(pair, gain.reshape(1, C), wl, wr)
+        [
+            pl.BlockSpec((M, half, ROWS, width), lambda i: (0, 0, i, 0)),
+            pl.BlockSpec((half, ROWS, J), lambda i: (0, i, 0)),
+        ],
+        [
+            jax.ShapeDtypeStruct((M, half, K, width), BF16),
+            jax.ShapeDtypeStruct((half, K, J), BF16),
+        ],
+        [pltpu.VMEM((half, ROWS, J), F32), pltpu.VMEM((half, ROWS, J), F32)],
+        [pair, gain.reshape(1, C), wl, wr],
+        comm,
+        cid,
+    )
 
 
 def contract_kernel(S, w, add, which_ref, l_ref, r_ref, *rest):
@@ -144,7 +270,7 @@
     lax.fori_loop(0, x_ref.shape[0], step, 0)
 
 
-def finish(v0, v1, pair, gain_in, gain_out, wg, wo, base, before):
+def finish(v0, v1, pair, gain_in, gain_out, wg, wo, base, before, comm=(), cid=None):
     K, J, C = pair.shape
     half, w, _ = v0.shape
     fixed = lambda i: (0, 0)
@@ -165,19 +291,18 @@
         in_specs.append(pl.BlockSpec(memory_space=pl.ANY))
         aliases = {len(operands): 0}
         operands.append(before)
-    return pl.pallas_call(
+    return call(
         finish_kernel,
-        grid=(w // ROWS,),
-        in_specs=in_specs,
-        out_specs=xspec,
-        out_shape=jax.ShapeDtypeStruct((K, J, C), BF16),
-        scratch_shapes=[pltpu.VMEM((C, ROWS, J), F32)],
-        input_output_aliases=aliases,
-        compiler_params=pltpu.CompilerParams(vmem_limit_bytes=VMEM_LIMIT),
-        cost_estimate=pl.CostEstimate(
-            flops=4 * w * J * C * C, bytes_accessed=6 * w * J * C, transcendentals=w * J * C
-        ),
-    )(*operands)
+        (w // ROWS,),
+        in_specs,
+        [xspec],
+        [jax.ShapeDtypeStruct((K, J, C), BF16)],
+        [pltpu.VMEM((C, ROWS, J), F32)],
+        operands,
+        comm,
+        cid,
+        aliases,
+    )
 
 
 def local(rlo, ncol, pair, gain_in, w_a_gate, w_a, w_b_gate, w_b, w_out_gate, w_out, gain_out):
@@ -190,54 +315,68 @@
     g = half // D
     h = lax.axis_index("half").astype(jnp.int32)
     mine, other = h.reshape(1), (1 - h).reshape(1)
-    swap = [(0, 1), (1, 0)]
-
-    wl = jnp.concatenate([w_a_gate.T, w_a.T], axis=0)
-    wr = jnp.concatenate([w_b_gate.T, w_b.T], axis=0)
-    l0, l1, r0, r1 = front(pair, gain_in, wl, wr, S, M, w)
-    lefts, rights = (l0, l1), (r0, r1)
-
-    def spread(block):
-        got = lax.all_to_all(block.reshape(D, g, K, -1), GROUP, 0, 0)
-        return got.reshape(rlo, ncol, g, K, -1)
-
-    def tie(value, after):
-        return value if after is None else lax.optimization_barrier((value, after))[0]
+
+    def weights(gate, value, q):
+        part = slice(q * half, (q + 1) * half)
+        return jnp.concatenate([gate[:, part].T, value[:, part].T], axis=0)
+
+    def project(q, comm=(), cid=None):
+        wl, wr = weights(w_a_gate, w_a, q), weights(w_b_gate, w_b, q)
+        return front(pair, gain_in, wl, wr, S, M, w, comm, cid)
+
+    def grouped(block):
+        return block.reshape(D, g, -1, block.shape[-1])
+
+    def received(block):
+        return block.reshape(rlo, ncol, g, K, -1)
+
+    def closing(m, out, comm=(), cid=None):
+        v0, v1 = back[m].reshape(half, w, J), back[M + m].reshape(half, w, J)
+        return finish(
+            v0, v1, pair, gain_in, gain_out, w_out_gate, w_out, m * w, out, comm, cid
+        )
 
     items = [(q, m) for q in range(2) for m in range(M)]
-    held_r, held_l, came, back = {}, {}, {}, {}
-    out = None
-
-    def prepare(t, after):
+    T = len(items)
+    lefts, rights, held_r, held_l, back = {}, {}, {}, {}, {}
+    lefts[0], rights[0] = project(0)
+    comm = [("spread", grouped(rights[0])), ("spread", grouped(lefts[0][0]))]
+    lefts[1], rights[1], got_r, got_l = project(1, comm, 0)
+    held_r[0], held_l[0] = received(got_r), received(got_l)
+    parts = [grouped(rights[1])[:, i * g // M : (i + 1) * g // M] for i in range(M)]
+    parts = [part for part in parts if part.shape[1]]
+    got_parts = []
+    out, total = None, None
+    for t in range(T):
         q, m = items[t]
-        if q not in held_r:
-            held_r[q] = spread(tie(rights[q], after))
-        held_l[t] = spread(tie(lefts[q][m], after))
-        sent = contract(other, held_l[t], held_r[q], S, w)
-        came[t] = lax.ppermute(sent, "half", swap)
-        return sent
-
-    def consume(t, after):
-        nonlocal out
-        q, m = items[t]
-        total = contract(mine, held_l.pop(t), held_r[q], S, w, came.pop(t), after)
-        ret = lax.all_to_all(total.reshape(D, g, w, J), GROUP, 0, 0)
-        back[t] = ret.reshape(half, w, J)
-        if q == 1:
-            out = finish(
-                back.pop(m), back.pop(t), pair, gain_in, gain_out, w_out_gate, w_out, m * w, out
-            )
-        return total
-
-    last = prepare(0, None)
-    last = prepare(1, last)
-    held_r[1] = spread(tie(rights[1], last))
-    for t in range(len(items)):
-        done = consume(t, last)
-        if t + 2 < len(items):
-            last = prepare(t + 2, done)
+        comm = [("swap", contract(other, held_l[t], held_r[q], S, w))]
+        names = ["swap"]
+        if total is not None:
+            comm.append(("spread", total.reshape(D, g, w, J)))
+            names.append("back")
+        if t + 1 < T:
+            nq, nm = items[t + 1]
+            comm.append(("spread", grouped(lefts[nq][nm])))
+            names.append("left")
+        if t < len(parts):
+            comm.append(("spread", parts[t]))
+            names.append("right")
+        if t >= M + 2:
+            out, *got = closing(t - M - 2, out, comm, t + 1)
         else:
-            last = None
+            got = call(None, (1,), [], [], [], [], [], comm, t + 1)
+        got = dict(zip(names, got))
+        if "back" in got:
+            back[t - 1] = got["back"]
+        if "left" in got:
+            held_l[t + 1] = received(got["left"])
+        if "right" in got:
+            got_parts.append(got["right"])
+            if len(got_parts) == len(parts):
+                held_r[1] = received(jnp.concatenate(got_parts, axis=1))
+        total = contract(mine, held_l.pop(t), held_r[q], S, w, got["swap"])
+    out, back[T - 1] = closing(M - 2, out, [("spread", total.reshape(D, g, w, J))], T + 1)
+    (out,) = closing(M - 1, out)
     return out
 
 

time: 1640 us -> 1590 us (0.970)
  Pallas kernels: 317 us -> 1530 us
  waiting for transfers between devices: 950 us -> 0 us
  blocking collectives: 286 us -> 0 us
  starting transfers between devices: 57.8 us -> 0 us
    pallas_call x4 -> x10, Pallas kernels: 216 us -> 1430 us  [call(): pl.pallas_call(body, grid=grid, in_specs=[*in_specs, *[anywhere] * n], ou...]
    ppermute x6 -> x0, waiting for transfers between devices: 693 us -> none  [prepare(): came[t] = lax.ppermute(sent, 'half', swap)]
    all_to_all x5 -> x0, blocking collectives: 286 us -> none  [spread(): got = lax.all_to_all(block.reshape(D, g, K, -1), GROUP, 0, 0)]
    all_to_all x9 -> x0, waiting for transfers between devices: 257 us -> none  [the longest x3 257 us: spread(): got = lax.all_to_all(block.reshape(D, g, K, -1), GROUP, 0, 0)]
    all_to_all x9 -> x0, starting transfers between devices: 38.5 us -> none  [the longest x6 23.9 us: consume(): ret = lax.all_to_all(total.reshape(D, g, w, J), GROUP, 0, 0)]
    slice x0 -> x8, local copies, waits for them, and re-layouts: none -> 25.2 us  [the longest x2 13.4 us: local(): comm.append(('spread', grouped(lefts[nq][nm])))]
    ppermute x6 -> x0, starting transfers between devices: 19.3 us -> none  [prepare(): came[t] = lax.ppermute(sent, 'half', swap)]
  transfers between devices with their start and end apart: 15 -> 0, of which waited for: 9 -> 0; matrix products, arithmetic and copies ran while one was open for 0% -> 0% of each run, Pallas kernels for 9% -> 0%
where the time goes in v2:
time: 1590 us; the launch traced here: 1580 us
  Pallas kernels  1530 us (96%)
  local copies, waits for them, and re-layouts  46.1 us (3%)
    pallas_call x10, Pallas kernels, call(): pl.pallas_call(body, grid=grid, in_specs=[*in_specs, *[anywhere] * n], ou...  1430 us
    pallas_call x12, Pallas kernels, contract(): pl.pallas_call(functools.partial(contract_kernel, S, w, got is not None),...  102 us

profile of v2, /device:TPU:0, one launch (start us, length us, event | category | flops | bytes accessed | tf_op | source)
XLA Modules:
  0.0 1582.2 jit_solution(11092345861321111905)
XLA Ops:
  0.0 1.4 copy.20.refs_4_
  2.5 0.9 fusion.6
  3.6 0.9 fusion.3
  4.7 0.9 fusion.4
  7.1 90.5 %shard_map.91 = (bf16[3,64,192,128]{3,2,1,0:T(8,128)(2,1)}, bf16[64,192,384]{2,1,0:T(8,128)(2,1)}) custom-call(bf16[192,384,128]{2,1,0:T(8,128)(2,1)} %refs_2_.5, f32[1,128]{1,0:T(1,128)} %bitcast.97, bf16[128,128]{1,0:T(8,128)(2,1)} %get-tuple-element.77.refs_2_, bf16[128,128]{1,0:T(8,128)(2,1)} %get-tuple-element.78.refs_3_), custom_call_target="tpu_custom_call" | custom-call | tf_op jit(solution)/shard_map/pallas_call | solution.py:149
  97.6 6.8 fusion.2
  104.3 191.8 %shard_map.92 = (bf16[3,64,192,128]{3,2,1,0:T(8,128)(2,1)}, bf16[64,192,384]{2,1,0:T(8,128)(2,1)}, bf16[16,4,192,384]{3,2,1,0:T(8,128)(2,1)}, bf16[16,4,192,128]{3,2,1,0:T(8,128)(2,1)}) custom-call(bf16[192,384,128]{2,1,0:T(8,128)(2,1)} %refs_2_.5, f32[1,128]{1,0:T(1,128)} %bitcast.98, bf16[128,128]{1,0:T(8,128)(2,1)} %get-tuple-element.79.refs_2_, ...), custom_call_target="tpu_custom_call" | custom-call | tf_op jit(solution)/shard_map/pallas_call | solution.py:149
  296.2 8.5 shard_map.93.refs_0_
  304.7 5.3 slice.70.refs_3_
  310.1 2.8 fusion.1
  312.8 148.4 %shard_map.94 = (bf16[4,4,4,64,384]{4,3,2,1,0:T(8,128)(2,1)}, bf16[16,4,192,128]{3,2,1,0:T(8,128)(2,1)}, bf16[16,1,192,384]{3,2,1,0:T(8,128)(2,1)}) custom-call(bf16[4,4,4,64,384]{4,3,2,1,0:T(8,128)(2,1)} %shard_map.93.refs_0_, bf16[16,4,192,128]{3,2,1,0:T(8,128)(2,1)} %bitcast.54, bf16[16,1,192,384]{3,2,1,0:T(8,128)(2,1)} %get-tuple-element.65.refs_2_), custom_call_target="tpu_custom_call" | custom-call | tf_op jit(solution)/shard_map/pallas_call | solution.py:149
  461.3 8.7 shard_map.96
  469.9 8.1 shard_map.95.refs_0_
  478.1 188.2 %shard_map.97 = (bf16[4,4,4,64,384]{4,3,2,1,0:T(8,128)(2,1)}, bf16[16,4,64,384]{3,2,1,0:T(8,128)(2,1)}, bf16[16,4,192,128]{3,2,1,0:T(8,128)(2,1)}, bf16[16,1,192,384]{3,2,1,0:T(8,128)(2,1)}) custom-call(bf16[4,4,4,64,384]{4,3,2,1,0:T(8,128)(2,1)} %shard_map.95.refs_0_, bf16[16,4,64,384]{3,2,1,0:T(8,128)(2,1)} %bitcast.74, ...), custom_call_target="tpu_custom_call" | custom-call | tf_op jit(solution)/shard_map/pallas_call | solution.py:149
  666.3 8.7 shard_map.99
  675.0 8.1 shard_map.98.refs_0_
  683.1 6.7 fusion
  689.8 233.3 %shard_map.100 = (bf16[4,4,4,64,384]{4,3,2,1,0:T(8,128)(2,1)}, bf16[16,4,64,384]{3,2,1,0:T(8,128)(2,1)}, bf16[16,4,192,128]{3,2,1,0:T(8,128)(2,1)}, bf16[16,2,192,384]{3,2,1,0:T(8,128)(2,1)}) custom-call(bf16[4,4,4,64,384]{4,3,2,1,0:T(8,128)(2,1)} %shard_map.98.refs_0_, bf16[16,4,64,384]{3,2,1,0:T(8,128)(2,1)} %bitcast.58, ...), custom_call_target="tpu_custom_call" | custom-call | tf_op jit(solution)/shard_map/pallas_call | solution.py:149
  923.2 9.6 shard_map.102
  932.8 6.0 pad_maximum_fusion
  938.8 8.1 shard_map.101.refs_0_
  946.9 176.9 %shard_map.103 = (bf16[4,4,4,64,384]{4,3,2,1,0:T(8,128)(2,1)}, bf16[16,4,64,384]{3,2,1,0:T(8,128)(2,1)}, bf16[16,4,192,128]{3,2,1,0:T(8,128)(2,1)}) custom-call(bf16[4,4,4,64,384]{4,3,2,1,0:T(8,128)(2,1)} %shard_map.101.refs_0_, bf16[16,4,64,384]{3,2,1,0:T(8,128)(2,1)} %bitcast.73, bf16[16,4,192,128]{3,2,1,0:T(8,128)(2,1)} %bitcast.57), custom_call_target="tpu_custom_call" | custom-call | tf_op jit(solution)/shard_map/pallas_call | solution.py:149
  1123.8 8.7 shard_map.105
  1132.4 8.1 shard_map.104.refs_0_
  1140.6 162.4 %shard_map.106 = (bf16[4,4,4,64,384]{4,3,2,1,0:T(8,128)(2,1)}, bf16[16,4,64,384]{3,2,1,0:T(8,128)(2,1)}, bf16[16,4,192,128]{3,2,1,0:T(8,128)(2,1)}) custom-call(bf16[4,4,4,64,384]{4,3,2,1,0:T(8,128)(2,1)} %shard_map.104.refs_0_, bf16[16,4,64,384]{3,2,1,0:T(8,128)(2,1)} %bitcast.75, bf16[16,4,192,128]{3,2,1,0:T(8,128)(2,1)} %bitcast.55), custom_call_target="tpu_custom_call" | custom-call | tf_op jit(solution)/shard_map/pallas_call | solution.py:149
  1303.0 8.7 shard_map.108
  1311.7 8.1 shard_map.107.refs_7_
  1319.8 141.9 %shard_map.109 = (bf16[192,384,128]{2,1,0:T(8,128)(2,1)}, bf16[4,4,4,64,384]{4,3,2,1,0:T(8,128)(2,1)}, bf16[16,4,64,384]{3,2,1,0:T(8,128)(2,1)}) custom-call(bf16[64,64,384]{2,1,0:T(8,128)(2,1)} %bitcast.85, bf16[64,64,384]{2,1,0:T(8,128)(2,1)} %bitcast.87, bf16[192,384,128]{2,1,0:T(8,128)(2,1)} %refs_2_.5, f32[1,128]{1,0:T(1,128)} %bitcast.99, ...), custom_call_target="tpu_custom_call" | custom-call | tf_op jit(solution)/shard_map/pallas_call | solution.py:149
  1461.8 8.7 shard_map.110
  1470.4 59.2 %shard_map.111 = (bf16[192,384,128]{2,1,0:T(8,128)(2,1)}, bf16[16,4,64,384]{3,2,1,0:T(8,128)(2,1)}) custom-call(bf16[64,64,384]{2,1,0:T(8,128)(2,1)} %bitcast.86, bf16[64,64,384]{2,1,0:T(8,128)(2,1)} %bitcast.88, bf16[192,384,128]{2,1,0:T(8,128)(2,1)} %refs_2_.5, f32[1,128]{1,0:T(1,128)} %bitcast.100, ...), custom_call_target="tpu_custom_call", output_to_operand_aliasing={{0}: (7, {})} | custom-call | tf_op jit(solution)/shard_map/pallas_call | solution.py:149
  1529.6 33.8 %shard_map.112 = bf16[192,384,128]{2,1,0:T(8,128)(2,1)} custom-call(bf16[64,64,384]{2,1,0:T(8,128)(2,1)} %bitcast.83, bf16[64,64,384]{2,1,0:T(8,128)(2,1)} %bitcast.84, bf16[192,384,128]{2,1,0:T(8,128)(2,1)} %refs_2_.5, f32[1,128]{1,0:T(1,128)} %bitcast.101, f32[128,1]{1,0:T(8,128)} %copy.20.refs_4_, ...), custom_call_target="tpu_custom_call", output_to_operand_aliasing={{}: (7, {})} | custom-call | tf_op jit(solution)/shard_map/pallas_call | solution.py:149
  1563.5 18.7 %copy.34 = bf16[192,384,128]{2,1,0:T(8,128)(2,1)} copy(bf16[192,384,128]{2,1,0:T(8,128)(2,1)} %shard_map.112) | data formatting | bytes 37748736
  (25 shorter events, 2.9 us)
Async XLA Ops:
  296.2 13.9 slice-start
  296.2 13.9 slice-start.1
  304.7 5.4 slice-start.2
  923.1 9.7 slice-start.3
  923.1 9.7 slice-start.4
  923.1 9.7 copy-start
